TPU v7x, 32 devices: a whole 2x2x4 slice. The times are simulated.
32 devices in a mesh: rows: 16 (over z, y, x), feat: 2 (over core).
Axes of the slice: x: 2, y: 2, z: 4, core: 2. Of those that a mesh axis runs over, the one named last changes fastest.
Arguments:
- descriptors: bfloat16 [4096, 128], P('rows'), may hold values from -6 to 6
- freqs: bfloat16 [128, 32768], P(None, 'feat'), may hold values from -0.5 to 0.5
- phases: float32 [32768], P('feat'), may hold values from -3.140625 to 3.140625
- row_weight: float32 [4096], P('rows'), may hold values from 0.3 to 15, as said below
- resid: float32 [4096, 128], P('rows'), may hold values from -6 to 6
- coef: float32 [32768, 128], P(('feat', 'rows')), may hold values from -4 to 4
- direction: float32 [32768, 128], P(('feat', 'rows')), may hold values from -6 to 6
- ridge: float32 [128], replicated, may hold values from 1 to 10
- gamma: float32 [128], replicated, may hold values from 300000 to 3000000
Outputs:
- coef_new: float32 [32768, 128], P(('feat', 'rows'))
- resid_new: float32 [4096, 128], P('rows')
- direction_new: float32 [32768, 128], P(('feat', 'rows'))
- gamma_new: float32 [128], replicated
Inputs may be any that keep to these rules, and one draw needn't show every extreme that they name: `row_weight`: positive weights of the profile rows.
All inputs are finite; a program needn't handle non-finite values.
Results may differ from a plain program's by a relative error of at most 0.0006.
The roundings to bfloat16 on the way count: a program that leaves them out, or rounds other values in their place, can miss the bound.
Values may be sent and summed in bfloat16 or wider, within the bound.
A program may use at most 64 MiB of HBM per device.

v0:
```python
import math

import jax
import jax.numpy as jnp
from jax import lax
from jax.sharding import PartitionSpec as P

FEAT = 32768


def make_features(block_x, freq_cols, phase_cols):
    scale = math.sqrt(2.0 / FEAT)
    angle = jnp.dot(block_x, freq_cols, preferred_element_type=jnp.float32) + phase_cols[None, :]
    return (scale * jnp.cos(angle)).astype(jnp.bfloat16)


def body(descriptors, freqs, phases, row_weight, resid, coef, direction, ridge, gamma):
    rows_dev = descriptors.shape[0]
    targets = resid.shape[1]
    block = min(256, rows_dev)
    empty = jnp.zeros((rows_dev, targets), jnp.float32)
    total = empty
    freq_cols = freqs
    phase_cols = phases
    feats = make_features(descriptors, freq_cols, phase_cols)
    update = jnp.dot(
        feats,
        lax.all_gather(direction.astype(jnp.bfloat16), "rows", axis=0, tiled=True),
        preferred_element_type=jnp.float32,
    )
    total = total.at[0:block].add(update)
    partial_image = total
    image = row_weight[:, None] * lax.psum(partial_image, "feat")
    step_local = jnp.sum(direction * direction, axis=0)
    image_sq = lax.psum(jnp.sum(image * image, axis=0), "rows")
    step_sq = lax.psum(step_local, ("rows", "feat"))
    curvature = image_sq + ridge * step_sq
    alpha = gamma / curvature
    coef_new = coef + alpha[None, :] * direction
    resid_new = resid - alpha[None, :] * image
    weighted_b = (row_weight[:, None] * resid_new).astype(jnp.bfloat16)
    own_count = coef.shape[0]
    freq_cols = freqs
    phase_cols = phases
    feats = make_features(descriptors, freq_cols, phase_cols)
    total = lax.dot_general(
        feats, weighted_b, (((0,), (0,)), ((), ())), preferred_element_type=jnp.float32
    )
    summed = lax.psum(total, "rows")
    mine = lax.dynamic_slice_in_dim(summed, lax.axis_index("rows") * own_count, own_count, 0)
    gradient = mine - ridge[None, :] * coef_new
    gamma_new = lax.psum(jnp.sum(gradient * gradient, axis=0), ("rows", "feat"))
    direction_new = gradient + (gamma_new / gamma)[None, :] * direction
    return (coef_new, resid_new, direction_new, gamma_new)


def solution(mesh):
    return jax.shard_map(
        body,
        mesh=mesh,
        in_specs=(
            P("rows", None),
            P(None, "feat"),
            P("feat"),
            P("rows"),
            P("rows", None),
            P(("feat", "rows"), None),
            P(("feat", "rows"), None),
            P(),
            P(),
        ),
        out_specs=(P(("feat", "rows"), None), P("rows", None), P(("feat", "rows"), None), P()),
        check_vma=False,
    )
```

profile of v0, /device:TPU:0, one launch (start us, length us, event | category | flops | bytes accessed | tf_op | source)
XLA Modules:
  0.0 490.2 jit_solution(15449940100342608273)
XLA Ops:
  7.2 0.0 copy-start
  7.2 0.0 all-gather.2.cloned.1.call-start
  7.2 2.1 multiply_reduce_fusion.1
  9.4 0.0 all-gather.2.cloned.1.call-update
  9.4 0.0 all-reduce.3.cloned.1.call-start
  9.4 0.0 copy-done
  9.5 58.7 %fusion.2 = bf16[256,16384]{1,0:T(8,128)(2,1)} fusion(bf16[256,128]{1,0:T(8,128)(2,1)S(1)} %copy-done, bf16[128,16384]{1,0:T(8,128)(2,1)} %param.14, f32[16384]{0:T(1024)} %param.15), kind=kOutput, calls=%fused_computation.3 | convolution fusion | flops 1086324736 | bytes 12713984 | tf_op jit(solution)/shard_map/dot_general | solution.py:13
  68.2 0.0 copy-start.6
  68.2 0.0 copy-start.7
  68.2 0.0 copy-start.8
  68.2 0.0 copy-start.5
  68.2 21.9 %all-gather.2.cloned.1.call-done = bf16[16384,128]{1,0:T(8,128)(2,1)} async-done(((bf16[1024,128]{1,0:T(8,128)(2,1)}), bf16[16384,128]{1,0:T(8,128)(2,1)}) %all-gather.2.cloned.1.call-update) | async-done | bytes 4194320 | tf_op jit(solution)/shard_map/all_gather | solution.py:28
  90.1 7.6 %fusion.5 = f32[256,128]{1,0:T(8,128)} fusion(bf16[256,16384]{1,0:T(8,128)(2,1)} %fusion.2, bf16[16384,128]{1,0:T(8,128)(2,1)} %all-gather.2.cloned.1.call-done), kind=kOutput, calls=%fused_computation.15 | convolution fusion | flops 1073741824 | bytes 12713984 | tf_op jit(solution)/shard_map/dot_general | solution.py:26
  97.7 0.0 all-reduce.3.cloned.1.call-update
  97.7 0.0 all-reduce.5.cloned.1.call-start
  97.8 39.3 %psum.37 = f32[128]{0:T(128)S(1)} all-reduce(f32[128]{0:T(128)S(1)} %get-tuple-element.26), channel_id=1, replica_groups=mesh['rows'=16,'feat'=2] {'rows','feat'}, use_global_device_ids=true, to_apply=%region_4.0 | all-reduce | flops 128 | bytes 1024 | tf_op jit(solution)/shard_map/psum | solution.py:36
  137.1 0.0 all-reduce.3.cloned.1.call-done
  137.1 0.0 copy-done.6
  137.1 1.0 multiply_reduce_fusion.2
  138.1 41.0 %psum.36 = f32[128]{0:T(128)S(1)} all-reduce(f32[128]{0:T(128)S(1)} %multiply_reduce_fusion.2), channel_id=1, replica_groups=mesh['rows'=16,'feat'=2] {'rows'}, use_global_device_ids=true, to_apply=%region_2.0 | all-reduce | flops 128 | bytes 1024 | tf_op jit(solution)/shard_map/psum | solution.py:35
  179.2 0.0 copy-done.7
  179.2 0.0 copy-done.8
  179.2 0.0 copy-done.5
  179.2 1.0 multiply_subtract_fusion.1
  180.2 0.0 copy-start.3
  180.2 9.1 %fusion.3 = f32[16384,128]{1,0:T(8,128)} fusion(bf16[256,16384]{1,0:T(8,128)(2,1)} %fusion.2, f32[256,128]{1,0:T(8,128)S(1)} %multiply_subtract_fusion.1, f32[256]{0:T(256)S(1)} %copy-done.6), kind=kOutput, calls=%fused_computation.12 | convolution fusion | flops 1073807360 | bytes 16909312 | tf_op jit(solution)/shard_map/dot_general | solution.py:46
  189.3 0.0 copy-done.3
  189.3 0.0 copy-start.1
  189.3 0.0 copy-start.4
  189.3 0.0 all-reduce.5.cloned.1.call-update
  189.3 252.3 %all-reduce.5.cloned.1.call-done = f32[16384,128]{1,0:T(8,128)} async-done(((f32[16384,128]{1,0:T(8,128)}), f32[16384,128]{1,0:T(8,128)}) %all-reduce.5.cloned.1.call-update) | async-done | bytes 8388624 | tf_op jit(solution)/shard_map/psum | solution.py:49
  441.6 0.0 copy-done.1
  441.6 0.0 copy-done.4
  441.6 1.2 multiply_reduce_fusion
  442.8 0.0 copy-start.2
  442.9 38.9 %psum.39 = f32[128]{0:T(128)S(1)} all-reduce(f32[128]{0:T(128)S(1)} %get-tuple-element.24), channel_id=1, replica_groups=mesh['rows'=16,'feat'=2] {'rows','feat'}, use_global_device_ids=true, to_apply=%region_7.0 | all-reduce | flops 128 | bytes 1024 | tf_op jit(solution)/shard_map/psum | solution.py:52
  481.7 0.0 copy-start.9
  481.7 1.9 multiply_add_fusion
  483.6 0.0 copy-done.2
  483.6 0.0 copy-done.9
  (2 shorter events, 0.0 us)
Async XLA Ops:
  7.2 2.3 copy-start
  7.2 83.0 %all-gather.2.cloned.1.call-start = ((), (), s32[]{:S(2)}) async-start(), calls=%async_computation | async-start | bytes 4456448 | tf_op jit(solution)/shard_map/all_gather | solution.py:28
  9.4 127.7 %all-reduce.3.cloned.1.call-start = ((), (), s32[]{:S(2)}) async-start(), calls=%async_computation.1 | async-start | bytes 262144 | tf_op jit(solution)/shard_map/psum | solution.py:33
  68.2 68.9 %copy-start.6 = (f32[256]{0:T(256)S(1)}, f32[256]{0:T(256)}, u32[]{:S(2)}) copy-start(f32[256]{0:T(256)} %param.16) | copy-start | bytes 3076
  68.2 111.0 %copy-start.7 = (f32[128]{0:T(128)S(1)}, f32[128]{0:T(128)}, u32[]{:S(2)}) copy-start(f32[128]{0:T(128)} %param.20) | copy-start | bytes 1540
  68.2 111.0 %copy-start.8 = (f32[128]{0:T(128)S(1)}, f32[128]{0:T(128)}, u32[]{:S(2)}) copy-start(f32[128]{0:T(128)} %param.21) | copy-start | bytes 1540
  68.2 111.0 %copy-start.5 = (f32[256,128]{1,0:T(8,128)S(1)}, f32[256,128]{1,0:T(8,128)}, u32[]{:S(2)}) copy-start(f32[256,128]{1,0:T(8,128)} %param.17) | copy-start | bytes 393220
  97.7 343.9 %all-reduce.5.cloned.1.call-start = ((), (), s32[]{:S(2)}) async-start(), calls=%async_computation.2 | async-start | bytes 16777216 | tf_op jit(solution)/shard_map/psum | solution.py:49
  180.2 9.1 %copy-start.3 = (f32[256,128]{1,0:T(8,128)}, f32[256,128]{1,0:T(8,128)S(1)}, u32[]{:S(2)}) copy-start(f32[256,128]{1,0:T(8,128)S(1)} %multiply_subtract_fusion.1) | copy-start | bytes 393220
  189.3 252.3 %copy-start.1 = (f32[1024,128]{1,0:T(8,128)S(1)}, f32[1024,128]{1,0:T(8,128)}, u32[]{:S(2)}) copy-start(f32[1024,128]{1,0:T(8,128)} %param.19) | copy-start | bytes 1572868
  189.3 252.3 %copy-start.4 = (f32[1024,128]{1,0:T(8,128)S(1)}, f32[1024,128]{1,0:T(8,128)}, u32[]{:S(2)}) copy-start(f32[1024,128]{1,0:T(8,128)} %param.18) | copy-start | bytes 1572868
  442.8 40.8 %copy-start.2 = (f32[1024,128]{1,0:T(8,128)}, f32[1024,128]{1,0:T(8,128)S(1)}, u32[]{:S(2)}) copy-start(f32[1024,128]{1,0:T(8,128)S(1)} %get-tuple-element.25) | copy-start | bytes 1572868
  481.7 1.9 copy-start.9
Sparse Core Ops, SparseCore 0:
  11.4 78.7 all-gather.1
  97.8 16.5 all-reduce.2
  189.4 252.1 all-reduce.4
where the time goes:
time: 491 us; the launch traced here: 490 us
  waiting for transfers between devices  274 us (56%)
  blocking collectives  119 us (24%)
  matrix products  75.4 us (15%)
  between operations  13.8 us (3%)
  other arithmetic  7.28 us (1%)
    psum x1, waiting for transfers between devices, body(): summed = lax.psum(total, 'rows')  252 us
    dot_general x1, matrix products, make_features(): jnp.dot(block_x, freq_cols, preferred_element_type=jnp.float32)  58.7 us
    psum x1, blocking collectives, body(): image_sq = lax.psum(jnp.sum(image * image, axis=0), 'rows')  41 us
    psum x1, blocking collectives, body(): step_sq = lax.psum(step_local, ('rows', 'feat'))  39.3 us
    psum x1, blocking collectives, body(): gamma_new = lax.psum(jnp.sum(gradient * gradient, axis=0), ('rows', 'feat'))  38.9 us
    all_gather x1, waiting for transfers between devices, body(): lax.all_gather(direction.astype(jnp.bfloat16), 'rows', axis=0, tiled=True)  21.9 us
  transfers between devices with their start and end apart: 3, of which 2 were waited for; matrix products, arithmetic and copies ran while one was open for 12% of the time, Pallas kernels for 0%

commit v1 on v0

v1 whole, which is shorter than its diff:
```python
import math

import jax
import jax.numpy as jnp
from jax import lax
from jax.sharding import PartitionSpec as P

FEAT = 32768


def make_features(block_x, freq_cols, phase_cols):
    scale = math.sqrt(2.0 / FEAT)
    angle = jnp.dot(block_x, freq_cols, preferred_element_type=jnp.float32) + phase_cols[None, :]
    return (scale * jnp.cos(angle)).astype(jnp.bfloat16)


def body(descriptors, freqs, phases, row_weight, resid, coef, direction, ridge, gamma):
    own = coef.shape[0]
    groups = lax.axis_size("feat")
    start = lax.axis_index("rows") * own
    freq_cols = lax.dynamic_slice_in_dim(freqs, start, own, 1)
    phase_cols = lax.dynamic_slice_in_dim(phases, start, own, 0)
    every = lax.all_gather(descriptors, "rows", axis=0, tiled=True)
    feats = make_features(every, freq_cols, phase_cols)
    part = jnp.dot(feats, direction.astype(jnp.bfloat16), preferred_element_type=jnp.float32)
    part = lax.psum_scatter(part, "rows", scatter_dimension=0, tiled=True)
    image = row_weight[:, None] * lax.psum(part, "feat")
    sums = jnp.stack([jnp.sum(image * image, axis=0) / groups, jnp.sum(direction * direction, axis=0)])
    sums = lax.psum(sums, ("rows", "feat"))
    alpha = gamma / (sums[0] + ridge * sums[1])
    coef_new = coef + alpha[None, :] * direction
    resid_new = resid - alpha[None, :] * image
    weighted_b = (row_weight[:, None] * resid_new).astype(jnp.bfloat16)
    weighted_b = lax.all_gather(weighted_b, "rows", axis=0, tiled=True)
    grad = lax.dot_general(
        feats, weighted_b, (((0,), (0,)), ((), ())), preferred_element_type=jnp.float32
    )
    gradient = grad - ridge[None, :] * coef_new
    gamma_new = lax.psum(jnp.sum(gradient * gradient, axis=0), ("rows", "feat"))
    direction_new = gradient + (gamma_new / gamma)[None, :] * direction
    return (coef_new, resid_new, direction_new, gamma_new)


def solution(mesh):
    return jax.shard_map(
        body,
        mesh=mesh,
        in_specs=(
            P("rows", None),
            P(None, "feat"),
            P("feat"),
            P("rows"),
            P("rows", None),
            P(("feat", "rows"), None),
            P(("feat", "rows"), None),
            P(),
            P(),
        ),
        out_specs=(P(("feat", "rows"), None), P("rows", None), P(("feat", "rows"), None), P()),
        check_vma=False,
    )
```

time: 491 us -> 382 us (0.78)
  waiting for transfers between devices: 274 us -> 213 us
  blocking collectives: 119 us -> 79.2 us
  matrix products: 75.4 us -> 67.4 us
    psum x2 -> x1, waiting for transfers between devices: 252 us -> 17.3 us  [body(): image = row_weight[:, None] * lax.psum(part, 'feat')]
    all_gather x1 -> x2, waiting for transfers between devices: 21.9 us -> 115 us  [the longest x1 60.1 us: body(): every = lax.all_gather(descriptors, 'rows', axis=0, tiled=True)]
    reduce_scatter x0 -> x1, waiting for transfers between devices: none -> 79.4 us  [body(): part = lax.psum_scatter(part, 'rows', scatter_dimension=0, tiled=True)]
    psum x2 -> x1, blocking collectives: 80.4 us -> 40.7 us  [body(): sums = lax.psum(sums, ('rows', 'feat'))]
  transfers between devices with their start and end apart: 3 -> 4, of which waited for: 2 -> 4; matrix products, arithmetic and copies ran while one was open for 12% -> 0% of each run, Pallas kernels for 0% -> 0%
where the time goes in v1:
time: 382 us; the launch traced here: 381 us
  waiting for transfers between devices  213 us (56%)
  blocking collectives  79.2 us (21%)
  matrix products  67.4 us (18%)
  between operations  13.9 us (4%)
  local copies, waits for them, and re-layouts  3.95 us (1%)
  other arithmetic  3.84 us (1%)
    reduce_scatter x1, waiting for transfers between devices, body(): part = lax.psum_scatter(part, 'rows', scatter_dimension=0, tiled=True)  79.4 us
    all_gather x1, waiting for transfers between devices, body(): every = lax.all_gather(descriptors, 'rows', axis=0, tiled=True)  60.1 us
    dot_general x1, matrix products, make_features(): jnp.dot(block_x, freq_cols, preferred_element_type=jnp.float32)  57.6 us
    all_gather x1, waiting for transfers between devices, body(): weighted_b = lax.all_gather(weighted_b, 'rows', axis=0, tiled=True)  55.1 us
    psum x1, blocking collectives, body(): sums = lax.psum(sums, ('rows', 'feat'))  40.7 us
    psum x1, blocking collectives, body(): gamma_new = lax.psum(jnp.sum(gradient * gradient, axis=0), ('rows', 'feat'))  38.5 us
    psum x1, waiting for transfers between devices, body(): image = row_weight[:, None] * lax.psum(part, 'feat')  17.3 us
  transfers between devices with their start and end apart: 4, of which 4 were waited for; matrix products, arithmetic and copies ran while one was open for 0% of the time, Pallas kernels for 0%

profile of v1, /device:TPU:0, one launch (start us, length us, event | category | flops | bytes accessed | tf_op | source)
XLA Modules:
  0.0 381.2 jit_solution(1640484167914621310)
XLA Ops:
  7.2 0.0 copy-start.1
  7.2 0.0 all-gather.3.cloned.1.call-start
  7.2 0.7 all-gather.3.cloned.1.call-update
  7.9 0.0 reduce-scatter.2.cloned.1.call-start
  8.0 0.7 dynamic_slice.7
  8.7 60.1 %all-gather.3.cloned.1.call-done = bf16[4096,128]{1,0:T(8,128)(2,1)} async-done(((bf16[256,128]{1,0:T(8,128)(2,1)}), bf16[4096,128]{1,0:T(8,128)(2,1)}) %all-gather.3.cloned.1.call-update) | async-done | bytes 1048592 | tf_op jit(solution)/shard_map/all_gather | solution.py:23
  68.8 57.6 %multiply_convert_fusion = bf16[1024,4096]{1,0:T(8,128)(2,1)S(1)} fusion(bf16[4096,128]{1,0:T(8,128)(2,1)} %all-gather.3.cloned.1.call-done, f32[1024]{0:T(1024)S(1)} %dynamic_slice.7, bf16[128,16384]{1,0:T(8,128)(2,1)} %param.10, s32[]{:T(128)S(6)} %select_n.4), kind=kOutput, calls=%fused_computation | convolution fusion | flops 1086324736 | bytes 9703428 | tf_op jit(solution)/shard_map/dot_general | solution.py:13
  126.4 0.0 copy-start
  126.4 3.2 copy-done
  129.7 0.0 copy-done.1
  129.7 0.0 copy-start.5
  129.7 0.0 copy-start.6
  129.7 0.0 copy-start.7
  129.7 0.0 copy-start.4
  129.7 0.0 copy-start.2
  129.7 3.8 %fusion = f32[4096,128]{1,0:T(8,128)} fusion(bf16[1024,4096]{1,0:T(8,128)(2,1)S(1)} %multiply_convert_fusion, f32[1024,128]{1,0:T(8,128)S(1)} %copy-done.1), kind=kOutput, calls=%fused_computation.6 | convolution fusion | flops 1073872896 | bytes 11010048 | tf_op jit(solution)/shard_map/dot_general | solution.py:25
  133.5 0.0 reduce-scatter.2.cloned.1.call-update
  133.6 0.0 all-reduce.2.cloned.1.call-start
  133.6 79.4 %reduce-scatter.2.cloned.1.call-done = f32[256,128]{1,0:T(8,128)} async-done(((f32[4096,128]{1,0:T(8,128)}), f32[256,128]{1,0:T(8,128)}) %reduce-scatter.2.cloned.1.call-update) | async-done | bytes 131088 | tf_op jit(solution)/shard_map/reduce_scatter | solution.py:26
  213.1 0.0 all-reduce.2.cloned.1.call-update
  213.1 0.0 all-gather.5.cloned.1.call-start
  213.1 0.2 multiply_reduce_fusion.1
  213.3 17.3 %all-reduce.2.cloned.1.call-done = f32[256,128]{1,0:T(8,128)} async-done(((f32[256,128]{1,0:T(8,128)}), f32[256,128]{1,0:T(8,128)}) %all-reduce.2.cloned.1.call-update) | async-done | bytes 131088 | tf_op jit(solution)/shard_map/psum | solution.py:27
  230.6 0.0 copy-done.5
  230.6 1.0 multiply_reduce_fusion.2
  231.6 40.7 %psum.22 = f32[2,128]{1,0:T(2,128)S(1)} all-reduce(f32[2,128]{1,0:T(2,128)S(1)} %pad_maximum_fusion), channel_id=1, replica_groups=mesh['rows'=16,'feat'=2] {'rows','feat'}, use_global_device_ids=true, to_apply=%region_4.0 | all-reduce | flops 256 | bytes 2048 | tf_op jit(solution)/shard_map/psum | solution.py:29
  272.4 0.0 copy-done.6
  272.4 0.0 copy-done.7
  272.4 0.0 copy-done.4
  272.4 1.7 multiply_convert_fusion.1
  274.1 0.0 all-gather.5.cloned.1.call-update
  274.1 0.0 copy-done.2
  274.1 0.1 multiply_add_fusion.1
  274.2 0.0 copy-start.3
  274.2 55.1 %all-gather.5.cloned.1.call-done = bf16[4096,128]{1,0:T(8,128)(2,1)} async-done(((bf16[256,128]{1,0:T(8,128)(2,1)}), bf16[4096,128]{1,0:T(8,128)(2,1)}) %all-gather.5.cloned.1.call-update) | async-done | bytes 1048592 | tf_op jit(solution)/shard_map/all_gather | solution.py:34
  329.3 6.0 %multiply_reduce_fusion = (f32[128]{0:T(128)S(1)}, f32[1024,128]{1,0:T(8,128)S(1)}) fusion(f32[1024,128]{1,0:T(8,128)S(1)} %multiply_add_fusion.1, f32[128]{0:T(128)S(1)} %copy-done.6, bf16[1024,4096]{1,0:T(8,128)(2,1)} %copy-done, bf16[4096,128]{1,0:T(8,128)(2,1)} %all-gather.5.cloned.1.call-done), kind=kOutput, calls=%fused_computation.3 | convolution fusion | flops 1074265984 | bytes 10486784 | tf_op jit(solution)/shard_map/dot_general | solution.py:35
  335.3 38.5 %psum.23 = f32[128]{0:T(128)S(1)} all-reduce(f32[128]{0:T(128)S(1)} %get-tuple-element.6), channel_id=1, replica_groups=mesh['rows'=16,'feat'=2] {'rows','feat'}, use_global_device_ids=true, to_apply=%region_6.0 | all-reduce | flops 128 | bytes 1024 | tf_op jit(solution)/shard_map/psum | solution.py:39
  373.7 0.0 copy-start.8
  373.7 0.9 multiply_add_fusion
  374.6 0.0 copy-done.3
  374.6 0.0 copy-done.8
  (4 shorter events, 0.0 us)
Async XLA Ops:
  7.2 122.5 %copy-start.1 = (f32[1024,128]{1,0:T(8,128)S(1)}, f32[1024,128]{1,0:T(8,128)}, u32[]{:S(2)}) copy-start(f32[1024,128]{1,0:T(8,128)} %param.15) | copy-start | bytes 1572868
  7.2 61.6 %all-gather.3.cloned.1.call-start = ((), (), s32[]{:S(2)}) async-start(), calls=%async_computation.1 | async-start | bytes 1114112 | tf_op jit(solution)/shard_map/all_gather | solution.py:23
  7.9 205.2 %reduce-scatter.2.cloned.1.call-start = ((), (), s32[]{:S(2)}) async-start(), calls=%async_computation.2 | async-start | bytes 2228224 | tf_op jit(solution)/shard_map/reduce_scatter | solution.py:26
  126.4 3.2 copy-start
  129.7 100.9 %copy-start.5 = (f32[256]{0:T(256)S(1)}, f32[256]{0:T(256)}, u32[]{:S(2)}) copy-start(f32[256]{0:T(256)} %param.12) | copy-start | bytes 3076
  129.7 142.7 %copy-start.6 = (f32[128]{0:T(128)S(1)}, f32[128]{0:T(128)}, u32[]{:S(2)}) copy-start(f32[128]{0:T(128)} %param.16) | copy-start | bytes 1540
  129.7 142.7 %copy-start.7 = (f32[128]{0:T(128)S(1)}, f32[128]{0:T(128)}, u32[]{:S(2)}) copy-start(f32[128]{0:T(128)} %param.17) | copy-start | bytes 1540
  129.7 142.7 %copy-start.4 = (f32[256,128]{1,0:T(8,128)S(1)}, f32[256,128]{1,0:T(8,128)}, u32[]{:S(2)}) copy-start(f32[256,128]{1,0:T(8,128)} %param.13) | copy-start | bytes 393220
  129.7 144.4 %copy-start.2 = (f32[1024,128]{1,0:T(8,128)S(1)}, f32[1024,128]{1,0:T(8,128)}, u32[]{:S(2)}) copy-start(f32[1024,128]{1,0:T(8,128)} %param.14) | copy-start | bytes 1572868
  133.6 97.0 %all-reduce.2.cloned.1.call-start = ((), (), s32[]{:S(2)}) async-start(), calls=%async_computation.3 | async-start | bytes 262144 | tf_op jit(solution)/shard_map/psum | solution.py:27
  213.1 116.3 %all-gather.5.cloned.1.call-start = ((), (), s32[]{:S(2)}) async-start(), calls=%async_computation.4 | async-start | bytes 1114112 | tf_op jit(solution)/shard_map/all_gather | solution.py:34
  274.2 100.4 %copy-start.3 = (f32[1024,128]{1,0:T(8,128)}, f32[1024,128]{1,0:T(8,128)S(1)}, u32[]{:S(2)}) copy-start(f32[1024,128]{1,0:T(8,128)S(1)} %multiply_add_fusion.1) | copy-start | bytes 1572868
  373.7 0.9 copy-start.8
Sparse Core Ops, SparseCore 0:
  10.8 57.9 all-gather.2
  133.7 79.3 reduce-scatter.1
  215.4 15.1 all-reduce.1
  274.2 55.0 all-gather.4

commit v2 on v1

--- a/solution.py
+++ b/solution.py
@@ -3,6 +3,8 @@
 import jax
 import jax.numpy as jnp
 from jax import lax
+from jax.experimental import pallas as pl
+from jax.experimental.pallas import tpu as pltpu
 from jax.sharding import PartitionSpec as P
 
 FEAT = 32768
@@ -41,9 +43,273 @@
     return (coef_new, resid_new, direction_new, gamma_new)
 
 
+STEPS = 4
+SLOTS = 16
+MESH = pl.DeviceIdType.MESH
+SINE = (0.04908738285303116, -0.32298168540000916, 0.6375077962875366, -0.598044216632843, 0.3088735342025757)
+
+
+def scaled_cos(angle):
+    turns = angle * 0.15915493667125702
+    v = 0.25 - jnp.abs(turns - jnp.round(turns))
+    s = v * v
+    p = SINE[4]
+    for c in SINE[3::-1]:
+        p = p * s + c
+    return p * v
+
+
+def column(row):
+    return jnp.transpose(jnp.broadcast_to(row, (128, 128)))
+
+
+def kernel(
+    desc_ref, freqs_ref, phases_ref, weight_ref, resid_ref, coef_ref, direction_ref, ridge_ref, gamma_ref,
+    coef_out, resid_out, direction_out, gamma_out,
+    fbuf, descs, freqs_t, dir_t, phase8, phase_b, feats, img, got0, got1, got2, got3,
+    wb, grad, grad_got, resid_got, small_out, small_got, local_sem, send, recv,
+):
+    own = coef_ref.shape[0]
+    tiles = own // 256
+    r, c = lax.axis_index("rows"), lax.axis_index("feat")
+    bits = [lax.rem(r // m, 2) for m in (1, 2, 4, 8)]
+    plain = [r + m * (1 - 2 * b) for m, b in zip((1, 2, 4, 8), bits)]
+    d = 1 - c
+    order = (
+        d * plain[0] + c * plain[1],
+        d * plain[1] + c * plain[2],
+        d * plain[2] + c * plain[0],
+        plain[3],
+    )
+
+    barrier = pltpu.get_barrier_semaphore()
+    pl.semaphore_signal(barrier, inc=1, device_id=(r, 1 - c), device_id_type=MESH)
+    for p in plain:
+        pl.semaphore_signal(barrier, inc=1, device_id=(p, c), device_id_type=MESH)
+
+    def copy(src, dst, k, rows, core=None):
+        return pltpu.make_async_remote_copy(
+            src_ref=src, dst_ref=dst, send_sem=send.at[k], recv_sem=recv.at[k],
+            device_id=(rows, c if core is None else core), device_id_type=MESH,
+        )
+
+    fetch = pltpu.make_async_copy(
+        freqs_ref.at[:, pl.ds(pl.multiple_of(r * own, own), own)], fbuf, local_sem
+    )
+    fetch.start()
+    descs[pl.ds(0, 128), :] = desc_ref[pl.ds(pl.multiple_of(c * 128, 128), 128), :]
+    phase8[0] = phases_ref[pl.ds(pl.multiple_of(r * 8, 8), 8), :]
+    dir_t[0] = jnp.transpose(direction_ref[...]).astype(jnp.bfloat16)
+    fetch.wait()
+    freqs_t[0] = jnp.transpose(fbuf[...].astype(jnp.float32)).astype(jnp.bfloat16)
+
+    pl.semaphore_wait(barrier, 5)
+
+    def spread(buf, size, k, base):
+        return copy(buf.at[pl.ds(0, size)], buf.at[pl.ds(size, size)], base + k, order[3 - k])
+
+    gather = [spread(descs, 128 << k, k, 0) for k in range(STEPS)]
+    gather[0].start()
+    swap = [
+        copy(phase8.at[0], phase8.at[1], 4, r, 1 - c),
+        copy(freqs_t.at[0], freqs_t.at[1], 5, r, 1 - c),
+        copy(dir_t.at[0], dir_t.at[1], 6, r, 1 - c),
+    ]
+    for s in swap:
+        s.start()
+
+    def expand(h):
+        for j in range(8):
+            phase_b[h, pl.ds(128 * j, 128), :] = column(phase8[h, pl.ds(j, 1), :])
+
+    expand(0)
+    weight = column(weight_ref[pl.ds(c, 1), :])
+    direction_sq = jnp.sum(direction_ref[...] * direction_ref[...], axis=0, keepdims=True)
+    gather[0].wait()
+    gather[1].start()
+    swap[0].wait()
+    expand(1)
+    swap[1].wait()
+    swap[2].wait()
+
+    def scatter0(b):
+        return copy(img.at[pl.ds(2 * b, 2)], got0.at[pl.ds(2 * (b - 4), 2)], 4 + b, order[0])
+
+    scatter1 = copy(img.at[pl.ds(4, 4)], got1, 12, order[1])
+
+    def block(i, carry):
+        @pl.when(i == 1)
+        def _():
+            gather[1].wait()
+            gather[2].start()
+
+        @pl.when(i == 2)
+        def _():
+            gather[2].wait()
+            gather[3].start()
+
+        @pl.when(i == 4)
+        def _():
+            gather[3].wait()
+
+        far = i // 4
+        b = far * (4 + lax.rem(i + 2, 4)) + (1 - far) * i
+        x = descs[pl.ds(pl.multiple_of(b * 256, 256), 256), :]
+        acc = jnp.zeros((128, 256), jnp.float32)
+        for h in range(2):
+            for t in range(tiles):
+                rows = pl.ds(256 * t, 256)
+                a = lax.dot_general(
+                    freqs_t[h, rows, :], x, (((1,), (1,)), ((), ())), preferred_element_type=jnp.float32
+                )
+                ph = phase_b[h, rows, :]
+                f = scaled_cos(a + jnp.concatenate([ph, ph], axis=1)).astype(jnp.bfloat16)
+                feats[b, h, rows, :] = f
+                acc += jnp.dot(dir_t[h, :, rows], f, preferred_element_type=jnp.float32)
+        img[2 * b] = acc[:, :128]
+        img[2 * b + 1] = acc[:, 128:]
+
+        @pl.when(i >= 4)
+        def _():
+            scatter0(b).start()
+
+        return carry
+
+    lax.fori_loop(0, 8, block, 0)
+
+    for b in (6, 7):
+        scatter0(b).wait()
+    for j in range(4, 8):
+        img[j] = img[j] + got0[j]
+    scatter1.start()
+    for b in (4, 5):
+        scatter0(b).wait()
+    for j in (2, 3, 0, 1):
+        img[j] = img[j] + got0[j]
+    scatter1.wait()
+    for j in (2, 3):
+        img[j] = img[j] + got1[j]
+    scatter2 = copy(img.at[pl.ds(2, 2)], got2, 13, order[2])
+    scatter2.start()
+    for j in (0, 1):
+        img[j] = img[j] + got1[j]
+    scatter2.wait()
+    img[1] = img[1] + got2[1]
+    scatter3 = copy(img.at[1], got3, 14, order[3])
+    scatter3.start()
+    img[0] = img[0] + got2[0]
+    scatter3.wait()
+
+    def allsum(value, call):
+        small = jnp.broadcast_to(value, (8, 128)) if value.shape[0] == 1 else value
+        for k in range(5):
+            n = 5 * call + k
+            small_out[n] = small
+            rows, core = (r, 1 - c) if k == 0 else (plain[k - 1], c)
+            s = copy(small_out.at[n], small_got.at[n], 15 + n, rows, core)
+            s.start()
+            s.wait()
+            small = small + small_got[n]
+        return small
+
+    image = weight * jnp.transpose(img[0] + got3[...])
+    image_sq = jnp.sum(image * image, axis=0, keepdims=True)
+    first = lax.broadcasted_iota(jnp.int32, (8, 128), 0) == 0
+    sums = allsum(jnp.where(first, image_sq, direction_sq), 0)
+    ridge, gamma = ridge_ref[...], gamma_ref[...]
+    alpha = gamma / (sums[0:1] + ridge * sums[1:2])
+    half = pl.ds(pl.multiple_of(c * 128, 128), 128)
+    other = pl.ds(pl.multiple_of((1 - c) * 128, 128), 128)
+    resid = resid_ref[half, :] - alpha * image
+    wb[pl.ds(0, 128), :] = (weight * resid).astype(jnp.bfloat16)
+    wgather = [spread(wb, 128 << k, k, 25) for k in range(STEPS)]
+    wgather[0].start()
+    resid_out[half, :] = resid
+    resid_got[0] = resid
+    rswap = copy(resid_got.at[0], resid_got.at[1], 29, r, 1 - c)
+    rswap.start()
+    coef_out[...] = coef_ref[...] + alpha * direction_ref[...]
+
+    def gradient(h, blocks, fresh=False):
+        for t in range(tiles):
+            rows = pl.ds(256 * t, 256)
+            g = None if fresh else grad[h, rows, :]
+            for b in blocks:
+                p = jnp.dot(feats[b, h, rows, :], wb[pl.ds(256 * b, 256), :], preferred_element_type=jnp.float32)
+                g = p if g is None else g + p
+            grad[h, rows, :] = g
+
+    for k, blocks in ((0, (0,)), (1, (1,)), (2, (2, 3))):
+        wgather[k].wait()
+        wgather[k + 1].start()
+        for h in (1, 0):
+            gradient(h, blocks, fresh=k == 0)
+    wgather[3].wait()
+    gradient(1, (4, 5, 6, 7))
+    gswap = copy(grad.at[1], grad_got, 30, r, 1 - c)
+    gswap.start()
+    gradient(0, (4, 5, 6, 7))
+    rswap.wait()
+    resid_out[other, :] = resid_got[1]
+    gswap.wait()
+    total = grad[0] + grad_got[...] - ridge * coef_out[...]
+    grad[0] = total
+    gamma_new = allsum(jnp.sum(total * total, axis=0, keepdims=True), 1)[0:1]
+    gamma_out[...] = gamma_new
+    direction_out[...] = grad[0] + (gamma_new / gamma) * direction_ref[...]
+
+
+def kernel_body(descriptors, freqs, phases, row_weight, resid, coef, direction, ridge, gamma):
+    own, targets = coef.shape
+    bf, f32 = jnp.bfloat16, jnp.float32
+    vmem = pl.BlockSpec(memory_space=pltpu.VMEM)
+    outs = pl.pallas_call(
+        kernel,
+        out_shape=(
+            jax.ShapeDtypeStruct(coef.shape, f32),
+            jax.ShapeDtypeStruct(resid.shape, f32),
+            jax.ShapeDtypeStruct(direction.shape, f32),
+            jax.ShapeDtypeStruct((1, targets), f32),
+        ),
+        in_specs=[vmem, pl.BlockSpec(memory_space=pl.ANY)] + [vmem] * 7,
+        out_specs=(vmem,) * 4,
+        scratch_shapes=[
+            pltpu.VMEM((128, own), bf),
+            pltpu.VMEM((SLOTS * 128, 128), bf),
+            pltpu.VMEM((2, own, 128), bf),
+            pltpu.VMEM((2, 128, own), bf),
+            pltpu.VMEM((2, 8, 128), f32),
+            pltpu.VMEM((2, own, 128), f32),
+            pltpu.VMEM((SLOTS // 2, 2, own, 256), bf),
+            pltpu.VMEM((SLOTS, 128, 128), f32),
+            pltpu.VMEM((8, 128, 128), f32),
+            pltpu.VMEM((4, 128, 128), f32),
+            pltpu.VMEM((2, 128, 128), f32),
+            pltpu.VMEM((128, 128), f32),
+            pltpu.VMEM((SLOTS * 128, 128), bf),
+            pltpu.VMEM((2, own, 128), f32),
+            pltpu.VMEM((own, 128), f32),
+            pltpu.VMEM((2, 128, 128), f32),
+            pltpu.VMEM((10, 8, 128), f32),
+            pltpu.VMEM((10, 8, 128), f32),
+            pltpu.SemaphoreType.DMA,
+            pltpu.SemaphoreType.DMA((31,)),
+            pltpu.SemaphoreType.DMA((31,)),
+        ],
+        compiler_params=pltpu.CompilerParams(
+            collective_id=0, has_side_effects=True, vmem_limit_bytes=48 * 1024 * 1024
+        ),
+    )(
+        descriptors, freqs, phases.reshape(-1, 128), row_weight.reshape(2, 128), resid, coef, direction,
+        ridge.reshape(1, -1), gamma.reshape(1, -1),
+    )
+    return outs[0], outs[1], outs[2], outs[3].reshape(-1)
+
+
 def solution(mesh):
+    fits = mesh.shape["rows"] == SLOTS and mesh.shape["feat"] == 2
     return jax.shard_map(
-        body,
+        kernel_body if fits else body,
         mesh=mesh,
         in_specs=(
             P("rows", None),

time: 382 us -> 96.3 us (0.25)
  waiting for transfers between devices: 213 us -> 0 us
  Pallas kernels: 0 us -> 85.9 us
  blocking collectives: 79.2 us -> 0 us
  matrix products: 67.4 us -> 0 us
  between operations: 13.9 us -> 0.66 us
  local copies, waits for them, and re-layouts: 3.95 us -> 9.4 us
  other arithmetic: 3.84 us -> 0 us
    all_gather x2 -> x0, waiting for transfers between devices: 115 us -> none  [the longest x1 60.1 us: body(): every = lax.all_gather(descriptors, 'rows', axis=0, tiled=True)]
    pallas_call x0 -> x1, Pallas kernels: none -> 85.9 us  [kernel_body(): pl.pallas_call(kernel, out_shape=(jax.ShapeDtypeStruct(coef.shape, f32),...]
    reduce_scatter x1 -> x0, waiting for transfers between devices: 79.4 us -> none  [body(): part = lax.psum_scatter(part, 'rows', scatter_dimension=0, tiled=True)]
    psum x2 -> x0, blocking collectives: 79.2 us -> none  [the longest x1 40.7 us: body(): sums = lax.psum(sums, ('rows', 'feat'))]
    dot_general x3 -> x0, matrix products: 67.4 us -> none  [the longest x1 57.6 us: make_features(): jnp.dot(block_x, freq_cols, preferred_element_type=jnp.float32)]
    psum x1 -> x0, waiting for transfers between devices: 17.3 us -> none  [body(): image = row_weight[:, None] * lax.psum(part, 'feat')]
    unnamed x18 -> x20, local copies, waits for them, and re-layouts: 3.26 us -> 9.4 us
  transfers between devices with their start and end apart: 4 -> 0, of which waited for: 4 -> 0; matrix products, arithmetic and copies ran while one was open for 0% -> 0% of each run, Pallas kernels for 0% -> 0%
where the time goes in v2:
time: 96.3 us; the launch traced here: 95.9 us
  Pallas kernels  85.9 us (89%)
  local copies, waits for them, and re-layouts  9.4 us (10%)
    pallas_call x1, Pallas kernels, kernel_body(): pl.pallas_call(kernel, out_shape=(jax.ShapeDtypeStruct(coef.shape, f32),...  85.9 us
    unnamed x20, local copies, waits for them, and re-layouts  9.4 us

profile of v2, /device:TPU:0, one launch (start us, length us, event | category | flops | bytes accessed | tf_op | source)
XLA Modules:
  0.0 95.9 jit_solution(14034424440409024619)
XLA Ops:
  0.6 0.0 copy-start
  0.6 1.0 %copy-done = f32[1024,128]{1,0:T(8,128)S(1)} copy-done((f32[1024,128]{1,0:T(8,128)S(1)}, f32[1024,128]{1,0:T(8,128)}, u32[]{:S(2)}) %copy-start) | copy-done | bytes 524312
  1.7 0.0 copy-start.1
  1.7 1.0 %copy-done.1 = f32[1024,128]{1,0:T(8,128)S(1)} copy-done((f32[1024,128]{1,0:T(8,128)S(1)}, f32[1024,128]{1,0:T(8,128)}, u32[]{:S(2)}) %copy-start.1) | copy-done | bytes 524312
  2.7 0.0 copy-start.2
  2.7 0.9 copy-done.2
  3.6 0.0 copy-start.3
  3.6 0.8 copy-done.3
  4.5 0.0 copy-start.4
  4.5 0.8 copy-done.4
  5.3 0.0 copy-start.5
  5.3 0.7 copy-done.5
  6.0 0.0 copy-start.6
  6.0 0.7 copy-done.6
  6.6 0.0 copy-start.7
  6.6 0.7 copy-done.7
  7.3 85.9 %shard_map.120 = (f32[1024,128]{1,0:T(8,128)S(1)}, f32[256,128]{1,0:T(8,128)S(1)}, f32[1024,128]{1,0:T(8,128)S(1)}, f32[1,128]{1,0:T(1,128)S(1)}) custom-call(bf16[256,128]{1,0:T(8,128)(2,1)S(1)} %copy-done.3, bf16[128,16384]{1,0:T(8,128)(2,1)} %freqs_ref.1, f32[128,128]{1,0:T(8,128)S(1)} %bitcast.5, f32[2,128]{1,0:T(2,128)S(1)} %bitcast.6, ...), custom_call_target="tpu_custom_call" | custom-call | tf_op jit(solution)/shard_map/pallas_call | solution.py:266
  93.2 0.8 copy.17
  94.0 0.7 copy.18
  94.6 0.8 copy.19
  95.4 0.5 copy.20
Async XLA Ops:
  0.6 1.0 %copy-start = (f32[1024,128]{1,0:T(8,128)S(1)}, f32[1024,128]{1,0:T(8,128)}, u32[]{:S(2)}) copy-start(f32[1024,128]{1,0:T(8,128)} %coef_ref.1) | copy-start | bytes 1572868
  1.7 1.0 %copy-start.1 = (f32[1024,128]{1,0:T(8,128)S(1)}, f32[1024,128]{1,0:T(8,128)}, u32[]{:S(2)}) copy-start(f32[1024,128]{1,0:T(8,128)} %direction_ref.1) | copy-start | bytes 1572868
  2.7 0.9 copy-start.2
  3.6 0.8 copy-start.3
  4.5 0.8 copy-start.4
  5.3 0.7 copy-start.5
  6.0 0.7 copy-start.6
  6.6 0.7 copy-start.7

commit v3 on v1

--- a/solution.py
+++ b/solution.py
@@ -3,6 +3,8 @@
 import jax
 import jax.numpy as jnp
 from jax import lax
+from jax.experimental import pallas as pl
+from jax.experimental.pallas import tpu as pltpu
 from jax.sharding import PartitionSpec as P
 
 FEAT = 32768
@@ -41,9 +43,336 @@
     return (coef_new, resid_new, direction_new, gamma_new)
 
 
+STEPS = 4
+SLOTS = 16
+MESH = pl.DeviceIdType.MESH
+SINE = (0.04908738285303116, -0.32298168540000916, 0.6375077962875366, -0.598044216632843, 0.3088735342025757)
+
+
+def scaled_cos(angle):
+    turns = angle * 0.15915493667125702
+    v = 0.25 - jnp.abs(turns - jnp.round(turns))
+    s = v * v
+    p = SINE[4]
+    for c in SINE[3::-1]:
+        p = p * s + c
+    return p * v
+
+
+def column(row):
+    return jnp.transpose(jnp.broadcast_to(row, (128, 128)))
+
+
+def kernel(
+    desc_ref, freqs_ref, phases_ref, weight_ref, resid_ref, coef_ref, direction_ref, ridge_ref, gamma_ref,
+    coef_out, resid_out, direction_out, gamma_out,
+    fbuf, dbuf, cbuf, rbuf, wbuf, ridge_buf, gamma_buf,
+    descs, freqs_t, dir_t, phase8, phase_b, feats, img, got,
+    wb, grad, grad_got, resid_got, small, local_sem, send, recv,
+):
+    own = coef_ref.shape[0]
+    tiles = own // 256
+    r, c = lax.axis_index("rows"), lax.axis_index("feat")
+    bits = [lax.rem(r // m, 2) for m in (1, 2, 4, 8)]
+    x, y, z1, z2 = [m * (1 - 2 * b) for m, b in zip((1, 2, 4, 8), bits)]
+    d = 1 - c
+    order = (r + d * x + c * y, r + d * y + c * z1, r + d * z1 + c * x, r + z2)
+    plane = [(r + i * x + j * y, c + k * (1 - 2 * c)) for j in (0, 1) for i in (0, 1) for k in (0, 1)]
+    line = [(r + i * z1 + j * z2, c) for j in (0, 1) for i in (0, 1)]
+
+    barrier = pltpu.get_barrier_semaphore()
+    for p in plane[1:] + line[1:]:
+        pl.semaphore_signal(barrier, inc=1, device_id=p, device_id_type=MESH)
+
+    half = pl.ds(pl.multiple_of(c * 128, 128), 128)
+    other = pl.ds(pl.multiple_of((1 - c) * 128, 128), 128)
+    fetches = [
+        pltpu.make_async_copy(src, dst, local_sem.at[n])
+        for n, (src, dst) in enumerate(
+            (
+                (desc_ref.at[half], descs.at[pl.ds(0, 128)]),
+                (phases_ref.at[pl.ds(pl.multiple_of(r * 8, 8), 8)], phase8.at[0]),
+                (freqs_ref.at[:, pl.ds(pl.multiple_of(r * own, own), own)], fbuf),
+                (direction_ref, dbuf),
+                (weight_ref, wbuf),
+                (resid_ref.at[half], rbuf),
+                (coef_ref, cbuf),
+                (ridge_ref, ridge_buf),
+                (gamma_ref, gamma_buf),
+            )
+        )
+    ]
+    for f in fetches:
+        f.start()
+
+    def copy(src, dst, k, device):
+        return pltpu.make_async_remote_copy(
+            src_ref=src, dst_ref=dst, send_sem=send.at[k], recv_sem=recv.at[k],
+            device_id=device, device_id_type=MESH,
+        )
+
+    def level(slot):
+        return slot.bit_length() - 1
+
+    def gathered(buf, slot, base):
+        k = level(slot)
+        return copy(
+            buf.at[pl.ds(128 * (slot - (1 << k)), 128)], buf.at[pl.ds(128 * slot, 128)],
+            base + slot, (order[3 - k], c),
+        )
+
+    def forward(buf, slot, base):
+        first = 0 if slot == 0 else level(slot) + 1
+        for k in range(first, STEPS):
+            gathered(buf, slot + (1 << k), base).start()
+
+    def take(buf, slot, base, pass_on=True):
+        gathered(buf, slot, base).wait_recv()
+        if pass_on:
+            forward(buf, slot, base)
+
+    D, W, S, A, M = 0, 16, 32, 48, 68
+
+    fetches[0].wait()
+    fetches[1].wait()
+    fetches[2].wait()
+    freqs_t[0] = jnp.transpose(fbuf[...].astype(jnp.float32)).astype(jnp.bfloat16)
+    fetches[3].wait()
+    dir_t[0] = jnp.transpose(dbuf[...]).astype(jnp.bfloat16)
+    pl.semaphore_wait(barrier, 10)
+
+    forward(descs, 0, D)
+    mate = (r, 1 - c)
+    swap = [
+        copy(phase8.at[0], phase8.at[1], M, mate),
+        copy(freqs_t.at[0], freqs_t.at[1], M + 1, mate),
+        copy(dir_t.at[0], dir_t.at[1], M + 2, mate),
+    ]
+    for s in swap:
+        s.start()
+
+    def expand(h):
+        for j in range(8):
+            phase_b[h, pl.ds(128 * j, 128), :] = column(phase8[h, pl.ds(j, 1), :])
+
+    expand(0)
+    for f in fetches[4:]:
+        f.wait()
+    weight = column(wbuf[pl.ds(c, 1), :])
+    direction_sq = jnp.sum(dbuf[...] * dbuf[...], axis=0, keepdims=True)
+    take(descs, 1, D)
+    take(descs, 2, D)
+    swap[0].wait_recv()
+    expand(1)
+    swap[1].wait_recv()
+    swap[2].wait_recv()
+
+    def summed(slot):
+        return copy(img.at[slot], got.at[slot], S + slot, (order[3 - level(slot)], c))
+
+    def far(slot):
+        return copy(img.at[slot], got.at[slot], S + slot, (order[0], c))
+
+    def collect(slot, tops):
+        for k in tops:
+            summed(slot + (1 << k)).wait_recv()
+        total = img[slot]
+        for k in tops:
+            total = total + got[slot + (1 << k)]
+        if slot:
+            img[slot] = total
+            summed(slot).start()
+        return total
+
+    def block(i, carry):
+        @pl.when(i == 1)
+        def _():
+            for s in (4, 3, 5, 6):
+                take(descs, s, D)
+
+        @pl.when(i == 2)
+        def _():
+            take(descs, 7, D)
+            for s in (14, 15):
+                take(descs, s, D)
+
+        for step in (3, 4, 5):
+            @pl.when(i == step)
+            def _():
+                for s in (18 - 2 * step, 19 - 2 * step):
+                    take(descs, s, D)
+
+        near = 1 - (i + 6) // 8
+        b = near * i + (1 - near) * (9 - i)
+        rows_b = descs[pl.ds(pl.multiple_of(b * 256, 256), 256), :]
+        acc = jnp.zeros((128, 256), jnp.float32)
+        for h in range(2):
+            for t in range(tiles):
+                rows = pl.ds(256 * t, 256)
+                a = lax.dot_general(
+                    freqs_t[h, rows, :], rows_b, (((1,), (1,)), ((), ())), preferred_element_type=jnp.float32
+                )
+                ph = phase_b[h, rows, :]
+                f = scaled_cos(a + jnp.concatenate([ph, ph], axis=1)).astype(jnp.bfloat16)
+                feats[b, h, rows, :] = f
+                acc += jnp.dot(dir_t[h, :, rows], f, preferred_element_type=jnp.float32)
+        img[2 * b] = acc[:, :128]
+        img[2 * b + 1] = acc[:, 128:]
+
+        @pl.when(b >= 4)
+        def _():
+            far(2 * b + 1).start()
+            far(2 * b).start()
+
+        @pl.when(i == 6)
+        def _():
+            collect(7, (3,))
+            collect(6, (3,))
+
+        @pl.when(i == 7)
+        def _():
+            collect(5, (3,))
+            collect(4, (3,))
+
+        return carry
+
+    lax.fori_loop(0, 8, block, 0)
+    collect(3, (3, 2))
+    collect(2, (3, 2))
+    collect(1, (3, 2, 1))
+    own_img = collect(0, (3, 2, 1, 0))
+
+    def allsum(value, call):
+        for stage, group in ((0, plane), (1, line)):
+            small[call, stage, 0] = value
+            hops = [
+                copy(small.at[call, stage, 0], small.at[call, stage, j], A + 10 * call + 7 * stage + j - 1, group[j])
+                for j in range(1, len(group))
+            ]
+            for p in hops:
+                p.start()
+            for p in hops:
+                p.wait_recv()
+            terms = [small[call, stage, j] for j in range(len(group))]
+            while len(terms) > 1:
+                terms = [terms[j] + terms[j + 1] for j in range(0, len(terms), 2)]
+            value = terms[0]
+            for p in hops:
+                p.wait_send()
+        return value
+
+    image = weight * jnp.transpose(own_img)
+    image_sq = jnp.sum(image * image, axis=0, keepdims=True)
+    first = lax.broadcasted_iota(jnp.int32, (8, 128), 0) == 0
+    sums = allsum(jnp.where(first, image_sq, direction_sq), 0)
+    ridge, gamma = ridge_buf[...], gamma_buf[...]
+    alpha = gamma / (sums[0:1] + ridge * sums[1:2])
+    resid = rbuf[...] - alpha * image
+    wb[pl.ds(0, 128), :] = (weight * resid).astype(jnp.bfloat16)
+    forward(wb, 0, W)
+    resid_out[half, :] = resid
+    resid_got[0] = resid
+    rswap = copy(resid_got.at[0], resid_got.at[1], M + 3, mate)
+    rswap.start()
+    coef_out[...] = cbuf[...] + alpha * dbuf[...]
+
+    def gradient(h, t, blocks, fresh):
+        rows = pl.ds(256 * t, 256)
+        g = None if fresh else grad[h, rows, :]
+        for b in blocks:
+            p = jnp.dot(feats[b, h, rows, :], wb[pl.ds(256 * b, 256), :], preferred_element_type=jnp.float32)
+            g = p if g is None else g + p
+        grad[h, rows, :] = g
+
+    for s in (1, 2, 4, 3, 5, 6, 7):
+        take(wb, s, W)
+    for h in (1, 0):
+        for t in range(tiles):
+            gradient(h, t, (0, 1, 2, 3), True)
+    for s in range(8, 16):
+        take(wb, s, W, False)
+    gswap = [
+        copy(grad.at[1, pl.ds(256 * t, 256)], grad_got.at[pl.ds(256 * t, 256)], M + 4 + t, mate)
+        for t in range(tiles)
+    ]
+    for t in range(tiles):
+        gradient(1, t, (4, 5, 6, 7), False)
+        gswap[t].start()
+    for t in range(tiles):
+        gradient(0, t, (4, 5, 6, 7), False)
+    rswap.wait()
+    resid_out[other, :] = resid_got[1]
+    squares = jnp.zeros((1, 128), jnp.float32)
+    for t in range(tiles):
+        gswap[t].wait_recv()
+        rows = pl.ds(256 * t, 256)
+        total = grad[0, rows, :] + grad_got[rows, :] - ridge * coef_out[rows, :]
+        grad[0, rows, :] = total
+        squares += jnp.sum(total * total, axis=0, keepdims=True)
+    gamma_new = allsum(jnp.broadcast_to(squares, (8, 128)), 1)[0:1]
+    gamma_out[...] = gamma_new
+    direction_out[...] = grad[0] + (gamma_new / gamma) * dbuf[...]
+    for s in range(1, 16):
+        gathered(descs, s, D).wait_send()
+        gathered(wb, s, W).wait_send()
+        summed(s).wait_send()
+    for s in swap + gswap:
+        s.wait_send()
+
+
+def kernel_body(descriptors, freqs, phases, row_weight, resid, coef, direction, ridge, gamma):
+    own, targets = coef.shape
+    bf, f32 = jnp.bfloat16, jnp.float32
+    vmem = pl.BlockSpec(memory_space=pltpu.VMEM)
+    outs = pl.pallas_call(
+        kernel,
+        out_shape=(
+            jax.ShapeDtypeStruct(coef.shape, f32),
+            jax.ShapeDtypeStruct(resid.shape, f32),
+            jax.ShapeDtypeStruct(direction.shape, f32),
+            jax.ShapeDtypeStruct((1, targets), f32),
+        ),
+        in_specs=[pl.BlockSpec(memory_space=pltpu.HBM)] * 9,
+        out_specs=(vmem,) * 4,
+        scratch_shapes=[
+            pltpu.VMEM((128, own), bf),
+            pltpu.VMEM((own, 128), f32),
+            pltpu.VMEM((own, 128), f32),
+            pltpu.VMEM((128, 128), f32),
+            pltpu.VMEM((2, 128), f32),
+            pltpu.VMEM((1, 128), f32),
+            pltpu.VMEM((1, 128), f32),
+            pltpu.VMEM((SLOTS * 128, 128), bf),
+            pltpu.VMEM((2, own, 128), bf),
+            pltpu.VMEM((2, 128, own), bf),
+            pltpu.VMEM((2, 8, 128), f32),
+            pltpu.VMEM((2, own, 128), f32),
+            pltpu.VMEM((SLOTS // 2, 2, own, 256), bf),
+            pltpu.VMEM((SLOTS, 128, 128), f32),
+            pltpu.VMEM((SLOTS, 128, 128), f32),
+            pltpu.VMEM((SLOTS * 128, 128), bf),
+            pltpu.VMEM((2, own, 128), f32),
+            pltpu.VMEM((own, 128), f32),
+            pltpu.VMEM((2, 128, 128), f32),
+            pltpu.VMEM((2, 2, 8, 8, 128), f32),
+            pltpu.SemaphoreType.DMA((9,)),
+            pltpu.SemaphoreType.DMA((76,)),
+            pltpu.SemaphoreType.DMA((76,)),
+        ],
+        compiler_params=pltpu.CompilerParams(
+            collective_id=0, has_side_effects=True, vmem_limit_bytes=48 * 1024 * 1024
+        ),
+    )(
+        descriptors, freqs, phases.reshape(-1, 128), row_weight.reshape(2, 128), resid, coef, direction,
+        ridge.reshape(1, -1), gamma.reshape(1, -1),
+    )
+    return outs[0], outs[1], outs[2], outs[3].reshape(-1)
+
+
 def solution(mesh):
+    fits = mesh.shape["rows"] == SLOTS and mesh.shape["feat"] == 2
     return jax.shard_map(
-        body,
+        kernel_body if fits else body,
         mesh=mesh,
         in_specs=(
             P("rows", None),

time: 382 us -> 76.2 us (0.20)
  waiting for transfers between devices: 213 us -> 0 us
  blocking collectives: 79.2 us -> 0 us
  matrix products: 67.4 us -> 0 us
  Pallas kernels: 0 us -> 65.8 us
  between operations: 13.9 us -> 0.66 us
  local copies, waits for them, and re-layouts: 3.95 us -> 9.4 us
  other arithmetic: 3.84 us -> 0 us
    all_gather x2 -> x0, waiting for transfers between devices: 115 us -> none  [the longest x1 60.1 us: body(): every = lax.all_gather(descriptors, 'rows', axis=0, tiled=True)]
    reduce_scatter x1 -> x0, waiting for transfers between devices: 79.4 us -> none  [body(): part = lax.psum_scatter(part, 'rows', scatter_dimension=0, tiled=True)]
    psum x2 -> x0, blocking collectives: 79.2 us -> none  [the longest x1 40.7 us: body(): sums = lax.psum(sums, ('rows', 'feat'))]
    dot_general x3 -> x0, matrix products: 67.4 us -> none  [the longest x1 57.6 us: make_features(): jnp.dot(block_x, freq_cols, preferred_element_type=jnp.float32)]
    pallas_call x0 -> x1, Pallas kernels: none -> 65.8 us  [kernel_body(): pl.pallas_call(kernel, out_shape=(jax.ShapeDtypeStruct(coef.shape, f32),...]
    psum x1 -> x0, waiting for transfers between devices: 17.3 us -> none  [body(): image = row_weight[:, None] * lax.psum(part, 'feat')]
    unnamed x18 -> x20, local copies, waits for them, and re-layouts: 3.26 us -> 9.4 us
  transfers between devices with their start and end apart: 4 -> 0, of which waited for: 4 -> 0; matrix products, arithmetic and copies ran while one was open for 0% -> 0% of each run, Pallas kernels for 0% -> 0%
where the time goes in v3:
time: 76.2 us; the launch traced here: 75.8 us
  Pallas kernels  65.8 us (86%)
  local copies, waits for them, and re-layouts  9.4 us (12%)
    pallas_call x1, Pallas kernels, kernel_body(): pl.pallas_call(kernel, out_shape=(jax.ShapeDtypeStruct(coef.shape, f32),...  65.8 us
    unnamed x20, local copies, waits for them, and re-layouts  9.4 us

profile of v3, /device:TPU:0, one launch (start us, length us, event | category | flops | bytes accessed | tf_op | source)
XLA Modules:
  0.0 75.8 jit_solution(3258438278021830785)
XLA Ops:
  0.6 0.0 copy-start
  0.6 1.0 %copy-done = f32[1024,128]{1,0:T(8,128)S(1)} copy-done((f32[1024,128]{1,0:T(8,128)S(1)}, f32[1024,128]{1,0:T(8,128)}, u32[]{:S(2)}) %copy-start) | copy-done | bytes 524312
  1.7 0.0 copy-start.1
  1.7 1.0 %copy-done.1 = f32[1024,128]{1,0:T(8,128)S(1)} copy-done((f32[1024,128]{1,0:T(8,128)S(1)}, f32[1024,128]{1,0:T(8,128)}, u32[]{:S(2)}) %copy-start.1) | copy-done | bytes 524312
  2.7 0.0 copy-start.2
  2.7 0.9 %copy-done.2 = f32[256,128]{1,0:T(8,128)S(1)} copy-done((f32[256,128]{1,0:T(8,128)S(1)}, f32[256,128]{1,0:T(8,128)}, u32[]{:S(2)}) %copy-start.2) | copy-done | bytes 131096
  3.6 0.0 copy-start.3
  3.6 0.8 %copy-done.3 = bf16[256,128]{1,0:T(8,128)(2,1)S(1)} copy-done((bf16[256,128]{1,0:T(8,128)(2,1)S(1)}, bf16[256,128]{1,0:T(8,128)(2,1)}, u32[]{:S(2)}) %copy-start.3) | copy-done | bytes 65560
  4.5 0.0 copy-start.4
  4.5 0.8 %copy-done.4 = f32[16384]{0:T(1024)S(1)} copy-done((f32[16384]{0:T(1024)S(1)}, f32[16384]{0:T(1024)}, u32[]{:S(2)}) %copy-start.4) | copy-done | bytes 65560
  5.3 0.0 copy-start.5
  5.3 0.7 copy-done.5
  6.0 0.0 copy-start.6
  6.0 0.7 copy-done.6
  6.6 0.0 copy-start.7
  6.6 0.7 copy-done.7
  7.3 65.8 %shard_map.120 = (f32[1024,128]{1,0:T(8,128)S(1)}, f32[256,128]{1,0:T(8,128)S(1)}, f32[1024,128]{1,0:T(8,128)S(1)}, f32[1,128]{1,0:T(1,128)S(1)}) custom-call(bf16[256,128]{1,0:T(8,128)(2,1)S(1)} %copy-done.3, bf16[128,16384]{1,0:T(8,128)(2,1)} %freqs_ref.1, f32[128,128]{1,0:T(8,128)S(1)} %bitcast.5, f32[2,128]{1,0:T(2,128)S(1)} %bitcast.6, ...), custom_call_target="tpu_custom_call" | custom-call | tf_op jit(solution)/shard_map/pallas_call | solution.py:327
  73.1 0.8 %copy.17 = f32[1024,128]{1,0:T(8,128)} copy(f32[1024,128]{1,0:T(8,128)S(1)} %get-tuple-element.16) | data formatting | bytes 1048576
  73.9 0.7 copy.18
  74.5 0.8 %copy.19 = f32[1024,128]{1,0:T(8,128)} copy(f32[1024,128]{1,0:T(8,128)S(1)} %get-tuple-element.18) | data formatting | bytes 1048576
  75.3 0.5 copy.20
Async XLA Ops:
  0.6 1.0 %copy-start = (f32[1024,128]{1,0:T(8,128)S(1)}, f32[1024,128]{1,0:T(8,128)}, u32[]{:S(2)}) copy-start(f32[1024,128]{1,0:T(8,128)} %coef_ref.1) | copy-start | bytes 1572868
  1.7 1.0 %copy-start.1 = (f32[1024,128]{1,0:T(8,128)S(1)}, f32[1024,128]{1,0:T(8,128)}, u32[]{:S(2)}) copy-start(f32[1024,128]{1,0:T(8,128)} %direction_ref.1) | copy-start | bytes 1572868
  2.7 0.9 %copy-start.2 = (f32[256,128]{1,0:T(8,128)S(1)}, f32[256,128]{1,0:T(8,128)}, u32[]{:S(2)}) copy-start(f32[256,128]{1,0:T(8,128)} %resid_ref.1) | copy-start | bytes 393220
  3.6 0.8 %copy-start.3 = (bf16[256,128]{1,0:T(8,128)(2,1)S(1)}, bf16[256,128]{1,0:T(8,128)(2,1)}, u32[]{:S(2)}) copy-start(bf16[256,128]{1,0:T(8,128)(2,1)} %desc_ref.1) | copy-start | bytes 196612
  4.5 0.8 %copy-start.4 = (f32[16384]{0:T(1024)S(1)}, f32[16384]{0:T(1024)}, u32[]{:S(2)}) copy-start(f32[16384]{0:T(1024)} %param.11) | copy-start | bytes 196612
  5.3 0.7 copy-start.5
  6.0 0.7 copy-start.6
  6.6 0.7 copy-start.7

commit v4 on v3

--- a/solution.py
+++ b/solution.py
@@ -46,11 +46,11 @@
 STEPS = 4
 SLOTS = 16
 MESH = pl.DeviceIdType.MESH
+TURN = 0.15915493667125702
 SINE = (0.04908738285303116, -0.32298168540000916, 0.6375077962875366, -0.598044216632843, 0.3088735342025757)
 
 
-def scaled_cos(angle):
-    turns = angle * 0.15915493667125702
+def scaled_cos(turns):
     v = 0.25 - jnp.abs(turns - jnp.round(turns))
     s = v * v
     p = SINE[4]
@@ -59,6 +59,13 @@
     return p * v
 
 
+def thirds(value):
+    a = value.astype(jnp.bfloat16)
+    rest = value - a.astype(jnp.float32)
+    b = rest.astype(jnp.bfloat16)
+    return a, b, (rest - b.astype(jnp.float32)).astype(jnp.bfloat16)
+
+
 def column(row):
     return jnp.transpose(jnp.broadcast_to(row, (128, 128)))
 
@@ -67,7 +74,7 @@
     desc_ref, freqs_ref, phases_ref, weight_ref, resid_ref, coef_ref, direction_ref, ridge_ref, gamma_ref,
     coef_out, resid_out, direction_out, gamma_out,
     fbuf, dbuf, cbuf, rbuf, wbuf, ridge_buf, gamma_buf,
-    descs, freqs_t, dir_t, phase8, phase_b, feats, img, got,
+    descs, freqs_t, dir_t, phase8, turn_t, feats, img, got,
     wb, grad, grad_got, resid_got, small, local_sem, send, recv,
 ):
     own = coef_ref.shape[0]
@@ -151,9 +158,17 @@
     for s in swap:
         s.start()
 
+    lane = lax.broadcasted_iota(jnp.int32, (128, 128), 1)
+
     def expand(h):
         for j in range(8):
-            phase_b[h, pl.ds(128 * j, 128), :] = column(phase8[h, pl.ds(j, 1), :])
+            rows = pl.ds(128 * j, 128)
+            terms = thirds(freqs_t[h, rows, :].astype(jnp.float32) * TURN)
+            for n in range(3):
+                turn_t[h, rows, pl.ds(128 * n, 128)] = terms[n]
+            terms = [t.astype(jnp.float32) for t in thirds(column(phase8[h, pl.ds(j, 1), :]) * TURN)]
+            last = jnp.where(lane == 0, terms[0], jnp.where(lane == 1, terms[1], jnp.where(lane == 2, terms[2], 0.0)))
+            turn_t[h, rows, pl.ds(384, 128)] = last.astype(jnp.bfloat16)
 
     expand(0)
     for f in fetches[4:]:
@@ -163,8 +178,8 @@
     take(descs, 1, D)
     take(descs, 2, D)
     swap[0].wait_recv()
+    swap[1].wait_recv()
     expand(1)
-    swap[1].wait_recv()
     swap[2].wait_recv()
 
     def summed(slot):
@@ -205,15 +220,15 @@
         near = 1 - (i + 6) // 8
         b = near * i + (1 - near) * (9 - i)
         rows_b = descs[pl.ds(pl.multiple_of(b * 256, 256), 256), :]
+        rows_b = jnp.concatenate([rows_b, rows_b, rows_b, jnp.ones_like(rows_b)], axis=1)
         acc = jnp.zeros((128, 256), jnp.float32)
         for h in range(2):
             for t in range(tiles):
                 rows = pl.ds(256 * t, 256)
                 a = lax.dot_general(
-                    freqs_t[h, rows, :], rows_b, (((1,), (1,)), ((), ())), preferred_element_type=jnp.float32
+                    turn_t[h, rows, :], rows_b, (((1,), (1,)), ((), ())), preferred_element_type=jnp.float32
                 )
-                ph = phase_b[h, rows, :]
-                f = scaled_cos(a + jnp.concatenate([ph, ph], axis=1)).astype(jnp.bfloat16)
+                f = scaled_cos(a).astype(jnp.bfloat16)
                 feats[b, h, rows, :] = f
                 acc += jnp.dot(dir_t[h, :, rows], f, preferred_element_type=jnp.float32)
         img[2 * b] = acc[:, :128]
@@ -346,7 +361,7 @@
             pltpu.VMEM((2, own, 128), bf),
             pltpu.VMEM((2, 128, own), bf),
             pltpu.VMEM((2, 8, 128), f32),
-            pltpu.VMEM((2, own, 128), f32),
+            pltpu.VMEM((2, own, 512), bf),
             pltpu.VMEM((SLOTS // 2, 2, own, 256), bf),
             pltpu.VMEM((SLOTS, 128, 128), f32),
             pltpu.VMEM((SLOTS, 128, 128), f32),
@@ -360,7 +375,7 @@
             pltpu.SemaphoreType.DMA((76,)),
         ],
         compiler_params=pltpu.CompilerParams(
-            collective_id=0, has_side_effects=True, vmem_limit_bytes=48 * 1024 * 1024
+            collective_id=0, has_side_effects=True, vmem_limit_bytes=62 * 1024 * 1024
         ),
     )(
         descriptors, freqs, phases.reshape(-1, 128), row_weight.reshape(2, 128), resid, coef, direction,

time: 76.2 us -> 75.3 us (0.988)
  local copies, waits for them, and re-layouts: 9.4 us -> 6.43 us
  Pallas kernels: 65.8 us -> 68 us
    unnamed x20 -> x4, local copies, waits for them, and re-layouts: 9.4 us -> 6.43 us
    pallas_call x1, Pallas kernels: 65.8 us -> 68 us  [kernel_body(): pl.pallas_call(kernel, out_shape=(jax.ShapeDtypeStruct(coef.shape, f32),...]
where the time goes in v4:
time: 75.3 us; the launch traced here: 75.1 us
  Pallas kernels  68 us (90%)
  local copies, waits for them, and re-layouts  6.43 us (9%)
    pallas_call x1, Pallas kernels, kernel_body(): pl.pallas_call(kernel, out_shape=(jax.ShapeDtypeStruct(coef.shape, f32),...  68 us
    unnamed x4, local copies, waits for them, and re-layouts  6.43 us

profile of v4, /device:TPU:0, one launch (start us, length us, event | category | flops | bytes accessed | tf_op | source)
XLA Modules:
  0.0 75.1 jit_solution(11907949917456167981)
XLA Ops:
  0.6 68.0 %shard_map.120 = (f32[1024,128]{1,0:T(8,128)}, f32[256,128]{1,0:T(8,128)}, f32[1024,128]{1,0:T(8,128)}, f32[1,128]{1,0:T(1,128)}) custom-call(bf16[256,128]{1,0:T(8,128)(2,1)} %desc_ref.1, bf16[128,16384]{1,0:T(8,128)(2,1)} %freqs_ref.1, f32[128,128]{1,0:T(8,128)} %bitcast.5, f32[2,128]{1,0:T(2,128)} %bitcast.6, f32[256,128]{1,0:T(8,128)} %resid_ref.1, ...), custom_call_target="tpu_custom_call" | custom-call | tf_op jit(solution)/shard_map/pallas_call | solution.py:342
  68.6 1.9 %copy.17 = f32[1024,128]{1,0:T(8,128)} copy(f32[1024,128]{1,0:T(8,128)} %get-tuple-element.16) | data formatting | bytes 1048576
  70.5 1.6 %copy.18 = f32[256,128]{1,0:T(8,128)} copy(f32[256,128]{1,0:T(8,128)} %get-tuple-element.17) | data formatting | bytes 262144
  72.1 1.9 %copy.19 = f32[1024,128]{1,0:T(8,128)} copy(f32[1024,128]{1,0:T(8,128)} %get-tuple-element.18) | data formatting | bytes 1048576
  73.9 1.1 %copy.20 = f32[128]{0:T(128)} copy(f32[128]{0:T(128)} %bitcast.9) | data formatting | bytes 1024

commit v5 on v4

--- a/solution.py
+++ b/solution.py
@@ -50,8 +50,9 @@
 SINE = (0.04908738285303116, -0.32298168540000916, 0.6375077962875366, -0.598044216632843, 0.3088735342025757)
 
 
-def scaled_cos(turns):
-    v = 0.25 - jnp.abs(turns - jnp.round(turns))
+def scaled_cos(angle):
+    turns = angle * TURN
+    v = 0.25 - jnp.abs(turns - ((turns + 12582912.0) - 12582912.0))
     s = v * v
     p = SINE[4]
     for c in SINE[3::-1]:
@@ -74,7 +75,7 @@
     desc_ref, freqs_ref, phases_ref, weight_ref, resid_ref, coef_ref, direction_ref, ridge_ref, gamma_ref,
     coef_out, resid_out, direction_out, gamma_out,
     fbuf, dbuf, cbuf, rbuf, wbuf, ridge_buf, gamma_buf,
-    descs, freqs_t, dir_t, phase8, turn_t, feats, img, got,
+    descs, freqs_t, dir_t, phase8, angle_t, feats, img, got,
     wb, grad, grad_got, resid_got, small, local_sem, send, recv,
 ):
     own = coef_ref.shape[0]
@@ -163,12 +164,10 @@
     def expand(h):
         for j in range(8):
             rows = pl.ds(128 * j, 128)
-            terms = thirds(freqs_t[h, rows, :].astype(jnp.float32) * TURN)
-            for n in range(3):
-                turn_t[h, rows, pl.ds(128 * n, 128)] = terms[n]
-            terms = [t.astype(jnp.float32) for t in thirds(column(phase8[h, pl.ds(j, 1), :]) * TURN)]
+            angle_t[h, rows, pl.ds(0, 128)] = freqs_t[h, rows, :]
+            terms = [t.astype(jnp.float32) for t in thirds(column(phase8[h, pl.ds(j, 1), :]))]
             last = jnp.where(lane == 0, terms[0], jnp.where(lane == 1, terms[1], jnp.where(lane == 2, terms[2], 0.0)))
-            turn_t[h, rows, pl.ds(384, 128)] = last.astype(jnp.bfloat16)
+            angle_t[h, rows, pl.ds(128, 128)] = last.astype(jnp.bfloat16)
 
     expand(0)
     for f in fetches[4:]:
@@ -220,13 +219,13 @@
         near = 1 - (i + 6) // 8
         b = near * i + (1 - near) * (9 - i)
         rows_b = descs[pl.ds(pl.multiple_of(b * 256, 256), 256), :]
-        rows_b = jnp.concatenate([rows_b, rows_b, rows_b, jnp.ones_like(rows_b)], axis=1)
+        rows_b = jnp.concatenate([rows_b, jnp.ones_like(rows_b)], axis=1)
         acc = jnp.zeros((128, 256), jnp.float32)
         for h in range(2):
             for t in range(tiles):
                 rows = pl.ds(256 * t, 256)
                 a = lax.dot_general(
-                    turn_t[h, rows, :], rows_b, (((1,), (1,)), ((), ())), preferred_element_type=jnp.float32
+                    angle_t[h, rows, :], rows_b, (((1,), (1,)), ((), ())), preferred_element_type=jnp.float32
                 )
                 f = scaled_cos(a).astype(jnp.bfloat16)
                 feats[b, h, rows, :] = f
@@ -361,7 +360,7 @@
             pltpu.VMEM((2, own, 128), bf),
             pltpu.VMEM((2, 128, own), bf),
             pltpu.VMEM((2, 8, 128), f32),
-            pltpu.VMEM((2, own, 512), bf),
+            pltpu.VMEM((2, own, 256), bf),
             pltpu.VMEM((SLOTS // 2, 2, own, 256), bf),
             pltpu.VMEM((SLOTS, 128, 128), f32),
             pltpu.VMEM((SLOTS, 128, 128), f32),
@@ -375,11 +374,16 @@
             pltpu.SemaphoreType.DMA((76,)),
         ],
         compiler_params=pltpu.CompilerParams(
-            collective_id=0, has_side_effects=True, vmem_limit_bytes=62 * 1024 * 1024
+            collective_id=0, has_side_effects=True, vmem_limit_bytes=48 * 1024 * 1024
         ),
     )(
-        descriptors, freqs, phases.reshape(-1, 128), row_weight.reshape(2, 128), resid, coef, direction,
-        ridge.reshape(1, -1), gamma.reshape(1, -1),
+        *(
+            pltpu.with_memory_space_constraint(a, pltpu.HBM)
+            for a in (
+                descriptors, freqs, phases.reshape(-1, 128), row_weight.reshape(2, 128), resid, coef, direction,
+                ridge.reshape(1, -1), gamma.reshape(1, -1),
+            )
+        )
     )
     return outs[0], outs[1], outs[2], outs[3].reshape(-1)
 

time: 75.3 us -> 70 us (0.930)
  local copies, waits for them, and re-layouts: 6.43 us -> 2.75 us
  Pallas kernels: 68 us -> 66.4 us
    unnamed x4, local copies, waits for them, and re-layouts: 6.43 us -> 2.75 us
    pallas_call x1, Pallas kernels: 68 us -> 66.4 us  [kernel_body(): pl.pallas_call(kernel, out_shape=(jax.ShapeDtypeStruct(coef.shape, f32),...]
where the time goes in v5:
time: 70 us; the launch traced here: 69.8 us
  Pallas kernels  66.4 us (95%)
  local copies, waits for them, and re-layouts  2.75 us (4%)
    pallas_call x1, Pallas kernels, kernel_body(): pl.pallas_call(kernel, out_shape=(jax.ShapeDtypeStruct(coef.shape, f32),...  66.4 us
    unnamed x4, local copies, waits for them, and re-layouts  2.75 us

profile of v5, /device:TPU:0, one launch (start us, length us, event | category | flops | bytes accessed | tf_op | source)
XLA Modules:
  0.0 69.8 jit_solution(10125266174254872376)
XLA Ops:
  0.6 66.4 %shard_map.120 = (f32[1024,128]{1,0:T(8,128)S(1)}, f32[256,128]{1,0:T(8,128)S(1)}, f32[1024,128]{1,0:T(8,128)S(1)}, f32[1,128]{1,0:T(1,128)S(1)}) custom-call(bf16[256,128]{1,0:T(8,128)(2,1)} %desc_ref.1, bf16[128,16384]{1,0:T(8,128)(2,1)} %freqs_ref.1, f32[128,128]{1,0:T(8,128)} %bitcast.6, f32[2,128]{1,0:T(2,128)} %bitcast.7, f32[256,128]{1,0:T(8,128)} %resid_ref.1, ...), custom_call_target="tpu_custom_call" | custom-call | tf_op jit(solution)/shard_map/pallas_call | solution.py:341
  67.1 0.8 %copy.17 = f32[1024,128]{1,0:T(8,128)} copy(f32[1024,128]{1,0:T(8,128)S(1)} %get-tuple-element.16) | data formatting | bytes 1048576
  67.9 0.7 copy.18
  68.5 0.8 %copy.19 = f32[1024,128]{1,0:T(8,128)} copy(f32[1024,128]{1,0:T(8,128)S(1)} %get-tuple-element.18) | data formatting | bytes 1048576
  69.3 0.5 copy.20

commit v6 on v5

--- a/solution.py
+++ b/solution.py
@@ -219,14 +219,13 @@
         near = 1 - (i + 6) // 8
         b = near * i + (1 - near) * (9 - i)
         rows_b = descs[pl.ds(pl.multiple_of(b * 256, 256), 256), :]
-        rows_b = jnp.concatenate([rows_b, jnp.ones_like(rows_b)], axis=1)
+        turned = jnp.transpose(rows_b.astype(jnp.float32)).astype(jnp.bfloat16)
+        turned = jnp.concatenate([turned, jnp.ones_like(turned)], axis=0)
         acc = jnp.zeros((128, 256), jnp.float32)
         for h in range(2):
-            for t in range(tiles):
-                rows = pl.ds(256 * t, 256)
-                a = lax.dot_general(
-                    angle_t[h, rows, :], rows_b, (((1,), (1,)), ((), ())), preferred_element_type=jnp.float32
-                )
+            for t in range(own // 512):
+                rows = pl.ds(512 * t, 512)
+                a = jnp.dot(angle_t[h, rows, :], turned, preferred_element_type=jnp.float32)
                 f = scaled_cos(a).astype(jnp.bfloat16)
                 feats[b, h, rows, :] = f
                 acc += jnp.dot(dir_t[h, :, rows], f, preferred_element_type=jnp.float32)
@@ -289,6 +288,11 @@
     rswap = copy(resid_got.at[0], resid_got.at[1], M + 3, mate)
     rswap.start()
     coef_out[...] = cbuf[...] + alpha * dbuf[...]
+    for s in range(1, 16):
+        gathered(descs, s, D).wait_send()
+        summed(s).wait_send()
+    for s in swap:
+        s.wait_send()
 
     def gradient(h, t, blocks, fresh):
         rows = pl.ds(256 * t, 256)
@@ -314,11 +318,13 @@
         gswap[t].start()
     for t in range(tiles):
         gradient(0, t, (4, 5, 6, 7), False)
+    for s in range(1, 16):
+        gathered(wb, s, W).wait_send()
     rswap.wait()
     resid_out[other, :] = resid_got[1]
     squares = jnp.zeros((1, 128), jnp.float32)
     for t in range(tiles):
-        gswap[t].wait_recv()
+        gswap[t].wait()
         rows = pl.ds(256 * t, 256)
         total = grad[0, rows, :] + grad_got[rows, :] - ridge * coef_out[rows, :]
         grad[0, rows, :] = total
@@ -326,12 +332,6 @@
     gamma_new = allsum(jnp.broadcast_to(squares, (8, 128)), 1)[0:1]
     gamma_out[...] = gamma_new
     direction_out[...] = grad[0] + (gamma_new / gamma) * dbuf[...]
-    for s in range(1, 16):
-        gathered(descs, s, D).wait_send()
-        gathered(wb, s, W).wait_send()
-        summed(s).wait_send()
-    for s in swap + gswap:
-        s.wait_send()
 
 
 def kernel_body(descriptors, freqs, phases, row_weight, resid, coef, direction, ridge, gamma):

time: 70 us -> 69.8 us (level)
  no operation moved by 1% of the time
where the time goes in v6:
time: 69.8 us; the launch traced here: 69.7 us
  Pallas kernels  66.3 us (95%)
  local copies, waits for them, and re-layouts  2.75 us (4%)
    pallas_call x1, Pallas kernels, kernel_body(): pl.pallas_call(kernel, out_shape=(jax.ShapeDtypeStruct(coef.shape, f32),...  66.3 us
    unnamed x4, local copies, waits for them, and re-layouts  2.75 us

profile of v6, /device:TPU:0, one launch (start us, length us, event | category | flops | bytes accessed | tf_op | source)
XLA Modules:
  0.0 69.7 jit_solution(12792520148138830172)
XLA Ops:
  0.6 66.3 %shard_map.120 = (f32[1024,128]{1,0:T(8,128)S(1)}, f32[256,128]{1,0:T(8,128)S(1)}, f32[1024,128]{1,0:T(8,128)S(1)}, f32[1,128]{1,0:T(1,128)S(1)}) custom-call(bf16[256,128]{1,0:T(8,128)(2,1)} %desc_ref.1, bf16[128,16384]{1,0:T(8,128)(2,1)} %freqs_ref.1, f32[128,128]{1,0:T(8,128)} %bitcast.6, f32[2,128]{1,0:T(2,128)} %bitcast.7, f32[256,128]{1,0:T(8,128)} %resid_ref.1, ...), custom_call_target="tpu_custom_call" | custom-call | tf_op jit(solution)/shard_map/pallas_call | solution.py:341
  66.9 0.8 %copy.17 = f32[1024,128]{1,0:T(8,128)} copy(f32[1024,128]{1,0:T(8,128)S(1)} %get-tuple-element.16) | data formatting | bytes 1048576
  67.7 0.7 copy.18
  68.4 0.8 %copy.19 = f32[1024,128]{1,0:T(8,128)} copy(f32[1024,128]{1,0:T(8,128)S(1)} %get-tuple-element.18) | data formatting | bytes 1048576
  69.1 0.5 copy.20

commit v7 on v6

--- a/solution.py
+++ b/solution.py
@@ -85,11 +85,14 @@
     x, y, z1, z2 = [m * (1 - 2 * b) for m, b in zip((1, 2, 4, 8), bits)]
     d = 1 - c
     order = (r + d * x + c * y, r + d * y + c * z1, r + d * z1 + c * x, r + z2)
-    plane = [(r + i * x + j * y, c + k * (1 - 2 * c)) for j in (0, 1) for i in (0, 1) for k in (0, 1)]
-    line = [(r + i * z1 + j * z2, c) for j in (0, 1) for i in (0, 1)]
+    both = (0, 1)
+    everyone = [
+        (r + i * x + j * y + k * z1 + n * z2, c + m * (1 - 2 * c))
+        for n in both for k in both for j in both for i in both for m in both
+    ]
 
     barrier = pltpu.get_barrier_semaphore()
-    for p in plane[1:] + line[1:]:
+    for p in everyone[1:]:
         pl.semaphore_signal(barrier, inc=1, device_id=p, device_id_type=MESH)
 
     half = pl.ds(pl.multiple_of(c * 128, 128), 128)
@@ -139,7 +142,7 @@
         if pass_on:
             forward(buf, slot, base)
 
-    D, W, S, A, M = 0, 16, 32, 48, 68
+    D, W, S, A, M = 0, 16, 32, 48, 110
 
     fetches[0].wait()
     fetches[1].wait()
@@ -147,7 +150,7 @@
     freqs_t[0] = jnp.transpose(fbuf[...].astype(jnp.float32)).astype(jnp.bfloat16)
     fetches[3].wait()
     dir_t[0] = jnp.transpose(dbuf[...]).astype(jnp.bfloat16)
-    pl.semaphore_wait(barrier, 10)
+    pl.semaphore_wait(barrier, 31)
 
     forward(descs, 0, D)
     mate = (r, 1 - c)
@@ -256,23 +259,21 @@
     own_img = collect(0, (3, 2, 1, 0))
 
     def allsum(value, call):
-        for stage, group in ((0, plane), (1, line)):
-            small[call, stage, 0] = value
-            hops = [
-                copy(small.at[call, stage, 0], small.at[call, stage, j], A + 10 * call + 7 * stage + j - 1, group[j])
-                for j in range(1, len(group))
-            ]
-            for p in hops:
-                p.start()
-            for p in hops:
-                p.wait_recv()
-            terms = [small[call, stage, j] for j in range(len(group))]
-            while len(terms) > 1:
-                terms = [terms[j] + terms[j + 1] for j in range(0, len(terms), 2)]
-            value = terms[0]
-            for p in hops:
-                p.wait_send()
-        return value
+        small[call, 0] = value
+        hops = [
+            copy(small.at[call, 0], small.at[call, j], A + 31 * call + j - 1, everyone[j])
+            for j in range(1, 32)
+        ]
+        for p in hops:
+            p.start()
+        for p in hops:
+            p.wait_recv()
+        terms = [small[call, j] for j in range(32)]
+        while len(terms) > 1:
+            terms = [terms[j] + terms[j + 1] for j in range(0, len(terms), 2)]
+        for p in hops:
+            p.wait_send()
+        return terms[0]
 
     image = weight * jnp.transpose(own_img)
     image_sq = jnp.sum(image * image, axis=0, keepdims=True)
@@ -368,10 +369,10 @@
             pltpu.VMEM((2, own, 128), f32),
             pltpu.VMEM((own, 128), f32),
             pltpu.VMEM((2, 128, 128), f32),
-            pltpu.VMEM((2, 2, 8, 8, 128), f32),
+            pltpu.VMEM((2, 32, 8, 128), f32),
             pltpu.SemaphoreType.DMA((9,)),
-            pltpu.SemaphoreType.DMA((76,)),
-            pltpu.SemaphoreType.DMA((76,)),
+            pltpu.SemaphoreType.DMA((118,)),
+            pltpu.SemaphoreType.DMA((118,)),
         ],
         compiler_params=pltpu.CompilerParams(
             collective_id=0, has_side_effects=True, vmem_limit_bytes=48 * 1024 * 1024

time: 69.8 us -> 69.6 us (level)
  no operation moved by 1% of the time
where the time goes in v7:
time: 69.6 us; the launch traced here: 69.4 us
  Pallas kernels  66 us (95%)
  local copies, waits for them, and re-layouts  2.75 us (4%)
    pallas_call x1, Pallas kernels, kernel_body(): pl.pallas_call(kernel, out_shape=(jax.ShapeDtypeStruct(coef.shape, f32),...  66 us
    unnamed x4, local copies, waits for them, and re-layouts  2.75 us

profile of v7, /device:TPU:0, one launch (start us, length us, event | category | flops | bytes accessed | tf_op | source)
XLA Modules:
  0.0 69.4 jit_solution(1492733609416556577)
XLA Ops:
  0.6 66.0 %shard_map.120 = (f32[1024,128]{1,0:T(8,128)S(1)}, f32[256,128]{1,0:T(8,128)S(1)}, f32[1024,128]{1,0:T(8,128)S(1)}, f32[1,128]{1,0:T(1,128)S(1)}) custom-call(bf16[256,128]{1,0:T(8,128)(2,1)} %desc_ref.1, bf16[128,16384]{1,0:T(8,128)(2,1)} %freqs_ref.1, f32[128,128]{1,0:T(8,128)} %bitcast.6, f32[2,128]{1,0:T(2,128)} %bitcast.7, f32[256,128]{1,0:T(8,128)} %resid_ref.1, ...), custom_call_target="tpu_custom_call" | custom-call | tf_op jit(solution)/shard_map/pallas_call | solution.py:342
  66.7 0.8 %copy.17 = f32[1024,128]{1,0:T(8,128)} copy(f32[1024,128]{1,0:T(8,128)S(1)} %get-tuple-element.16) | data formatting | bytes 1048576
  67.5 0.7 copy.18
  68.1 0.8 %copy.19 = f32[1024,128]{1,0:T(8,128)} copy(f32[1024,128]{1,0:T(8,128)S(1)} %get-tuple-element.18) | data formatting | bytes 1048576
  68.9 0.5 copy.20

commit v8 on v7

--- a/solution.py
+++ b/solution.py
@@ -126,16 +126,20 @@
         return slot.bit_length() - 1
 
     def gathered(buf, slot, base):
-        k = level(slot)
+        move = slot - slot % 4 if slot >= 4 else slot
+        to = r
+        for k in range(STEPS):
+            if move >> k & 1:
+                to = to + order[3 - k] - r
         return copy(
-            buf.at[pl.ds(128 * (slot - (1 << k)), 128)], buf.at[pl.ds(128 * slot, 128)],
-            base + slot, (order[3 - k], c),
+            buf.at[pl.ds(128 * (slot - move), 128)], buf.at[pl.ds(128 * slot, 128)], base + slot, (to, c)
         )
 
     def forward(buf, slot, base):
-        first = 0 if slot == 0 else level(slot) + 1
-        for k in range(first, STEPS):
-            gathered(buf, slot + (1 << k), base).start()
+        near = (1, 2, 3) if slot == 0 else ()
+        far_slots = (slot + 4, slot + 8, slot + 12) if slot < 4 else ()
+        for n in near + far_slots:
+            gathered(buf, n, base).start()
 
     def take(buf, slot, base, pass_on=True):
         gathered(buf, slot, base).wait_recv()
@@ -179,6 +183,7 @@
     direction_sq = jnp.sum(dbuf[...] * dbuf[...], axis=0, keepdims=True)
     take(descs, 1, D)
     take(descs, 2, D)
+    take(descs, 3, D)
     swap[0].wait_recv()
     swap[1].wait_recv()
     expand(1)
@@ -202,18 +207,7 @@
         return total
 
     def block(i, carry):
-        @pl.when(i == 1)
-        def _():
-            for s in (4, 3, 5, 6):
-                take(descs, s, D)
-
-        @pl.when(i == 2)
-        def _():
-            take(descs, 7, D)
-            for s in (14, 15):
-                take(descs, s, D)
-
-        for step in (3, 4, 5):
+        for step in range(2, 8):
             @pl.when(i == step)
             def _():
                 for s in (18 - 2 * step, 19 - 2 * step):
@@ -303,7 +297,7 @@
             g = p if g is None else g + p
         grad[h, rows, :] = g
 
-    for s in (1, 2, 4, 3, 5, 6, 7):
+    for s in range(1, 8):
         take(wb, s, W)
     for h in (1, 0):
         for t in range(tiles):

time: 69.6 us -> 65 us (0.934)
  Pallas kernels: 66 us -> 61.4 us
    pallas_call x1, Pallas kernels: 66 us -> 61.4 us  [kernel_body(): pl.pallas_call(kernel, out_shape=(jax.ShapeDtypeStruct(coef.shape, f32),...]
where the time goes in v8:
time: 65 us; the launch traced here: 64.8 us
  Pallas kernels  61.4 us (94%)
  local copies, waits for them, and re-layouts  2.75 us (4%)
    pallas_call x1, Pallas kernels, kernel_body(): pl.pallas_call(kernel, out_shape=(jax.ShapeDtypeStruct(coef.shape, f32),...  61.4 us
    unnamed x4, local copies, waits for them, and re-layouts  2.75 us

profile of v8, /device:TPU:0, one launch (start us, length us, event | category | flops | bytes accessed | tf_op | source)
XLA Modules:
  0.0 64.8 jit_solution(15921593464514040248)
XLA Ops:
  0.6 61.4 %shard_map.120 = (f32[1024,128]{1,0:T(8,128)S(1)}, f32[256,128]{1,0:T(8,128)S(1)}, f32[1024,128]{1,0:T(8,128)S(1)}, f32[1,128]{1,0:T(1,128)S(1)}) custom-call(bf16[256,128]{1,0:T(8,128)(2,1)} %desc_ref.1, bf16[128,16384]{1,0:T(8,128)(2,1)} %freqs_ref.1, f32[128,128]{1,0:T(8,128)} %bitcast.6, f32[2,128]{1,0:T(2,128)} %bitcast.7, f32[256,128]{1,0:T(8,128)} %resid_ref.1, ...), custom_call_target="tpu_custom_call" | custom-call | tf_op jit(solution)/shard_map/pallas_call | solution.py:336
  62.1 0.8 %copy.17 = f32[1024,128]{1,0:T(8,128)} copy(f32[1024,128]{1,0:T(8,128)S(1)} %get-tuple-element.16) | data formatting | bytes 1048576
  62.9 0.7 %copy.18 = f32[256,128]{1,0:T(8,128)} copy(f32[256,128]{1,0:T(8,128)S(1)} %get-tuple-element.17) | data formatting | bytes 262144
  63.5 0.8 %copy.19 = f32[1024,128]{1,0:T(8,128)} copy(f32[1024,128]{1,0:T(8,128)S(1)} %get-tuple-element.18) | data formatting | bytes 1048576
  64.3 0.5 copy.20
